TPU v7x, 32 devices: a whole 2x2x4 slice. The times are simulated.
32 devices in a mesh: groups: 2 (over y), psg: 16 (over z, x, core).
Axes of the slice: x: 2, y: 2, z: 4, core: 2. Of those that a mesh axis runs over, the one named last changes fastest.
Arguments:
- tail_hidden_states: bfloat16 [256, 8192], P('groups', 'psg'), parts along dimension 0, may hold values from -6 to 6
- passage_hidden_states: bfloat16 [2048, 8192], P(('groups', 'psg')), parts along dimension 0, may hold values from -6 to 6
- lengths: int32 [4], P('groups'), parts along dimension 0, may hold values from 1 to 768, 1024 in all
- storage_order: int32 [4], P('groups'), parts along dimension 0, may hold values from 0 to 1, each once
- orders: int32 [6, 2], P('groups'), parts along dimension 0, may hold values from 0 to 1, each once within a row
- w_query: bfloat16 [8192, 4096], P('psg'), may hold values from -1 to 1
- key_weight: bfloat16 [8192, 512], P('psg'), may hold values from -0.0625 to 0.0625
- value_weight: bfloat16 [8192, 512], P('psg'), may hold values from -0.0625 to 0.0625
- w_out: bfloat16 [4096, 8192], P(None, 'psg'), may hold values from -0.09375 to 0.09375
- norm_gain: float32 [8192], P('psg'), may hold values from 0.1 to 1.9
Outputs:
- layer_out: bfloat16 [256, 8192], P('groups', 'psg'), parts along dimension 0
There are 2 independent parts, one for each index of `groups`. A program takes and returns all parts, laid end to end along the dimension named above; an argument that names none is the same for every part. Nothing has to cross between parts.
Inputs may be any that keep to these rules, and one draw needn't show every extreme that they name: `lengths`: they sum to 1024; the largest is 768. `storage_order`: A permutation of the passages. `orders`: each row is a permutation of the passages.
All inputs are finite; a program needn't handle non-finite values.
Results may differ from a plain program's by a relative error of at most 0.01065.
The roundings to bfloat16 on the way count: a program that leaves them out, or rounds other values in their place, can miss the bound.
Values may be sent and summed in bfloat16 or wider, within the bound.
A program may use at most 128 MiB of HBM per device.

v0:
```python
import jax
import jax.numpy as jnp
from jax import lax
from jax.sharding import PartitionSpec as P

MODEL_WIDTH = 8192
HEAD_SIZE = 128


theta_base = 500000.0
epsilon = 1e-05


def joined(part, axis, combine):
    gathered = jax.tree.map(lambda a: lax.all_gather(a, axis), part)

    def take(source):
        return jax.tree.map(lambda a: lax.dynamic_index_in_dim(a, source, 0, False), gathered)

    return lax.fori_loop(
        1, lax.axis_size(axis), lambda source, state: combine(state, take(source)), take(0)
    )


def rotate(vectors, places):
    half = vectors.shape[-1] // 2
    freqs = theta_base ** (-jnp.arange(half, dtype=jnp.float32) * 2.0 / vectors.shape[-1])
    angles = places.astype(jnp.float32)[:, None] * freqs[None, :]
    cosine = jnp.cos(angles)[:, None, :]
    sine = jnp.sin(angles)[:, None, :]
    first = vectors[..., :half]
    second = vectors[..., half:]
    return jnp.concatenate(
        [first * cosine - second * sine, second * cosine + first * sine], axis=-1
    )


def per_device(
    tail_hidden_states,
    passage_hidden_states,
    lengths,
    storage_order,
    orders,
    w_query,
    key_weight,
    value_weight,
    w_out,
    norm_gain,
):
    shards = lax.axis_size("psg")
    device = lax.axis_index("psg")
    row_count = passage_hidden_states.shape[0]
    tail_count = tail_hidden_states.shape[0]
    kv_heads = key_weight.shape[1] // HEAD_SIZE
    query_heads = w_query.shape[1] // HEAD_SIZE
    query_group = query_heads // kv_heads
    total_keys = row_count * shards
    query_part = jnp.dot(tail_hidden_states, w_query, preferred_element_type=jnp.float32)
    key_part = jnp.dot(tail_hidden_states, key_weight, preferred_element_type=jnp.float32)
    value_part = jnp.dot(tail_hidden_states, value_weight, preferred_element_type=jnp.float32)
    query_sum, key_sum, value_sum = lax.psum((query_part, key_part, value_part), "psg")
    tail_pos = total_keys + jnp.arange(tail_count, dtype=jnp.int32)
    query_vectors = rotate(query_sum.reshape(tail_count, query_heads, HEAD_SIZE), tail_pos).astype(
        jnp.bfloat16
    )
    query_vectors = query_vectors.reshape(tail_count, kv_heads, query_group, HEAD_SIZE)
    tail_key_rows = rotate(key_sum.reshape(tail_count, kv_heads, HEAD_SIZE), tail_pos).astype(
        jnp.bfloat16
    )
    tail_value_rows = value_sum.astype(jnp.bfloat16).reshape(tail_count, kv_heads, HEAD_SIZE)

    def add_block(piece):
        return jnp.dot(passage_hidden_states, piece, preferred_element_type=jnp.float32)

    unrotated_key = add_block(lax.all_gather(key_weight, "psg", axis=0, tiled=True))
    raw_value = add_block(lax.all_gather(value_weight, "psg", axis=0, tiled=True))
    numbers = jnp.arange(lengths.shape[0], dtype=jnp.int32)
    pick = (storage_order[:, None] == numbers[None, :]).astype(jnp.int32)
    stored_lengths = jnp.sum(pick * lengths[None, :], axis=1)
    ends = jnp.cumsum(stored_lengths)
    starts = ends - stored_lengths
    row_ids = device * row_count + jnp.arange(row_count, dtype=jnp.int32)
    slots = jnp.sum((ends[None, :] <= row_ids[:, None]).astype(jnp.int32), axis=1)
    in_slot = (slots[:, None] == numbers[None, :]).astype(jnp.int32)
    offsets = row_ids - jnp.sum(in_slot * starts[None, :], axis=1)
    passage_hot = jnp.dot(in_slot, pick)
    ordered_hot = (orders[:, :, None] == numbers[None, None, :]).astype(jnp.int32)
    ordered_lengths = jnp.sum(ordered_hot * lengths[None, None, :], axis=2)
    order_starts = jnp.cumsum(ordered_lengths, axis=1) - ordered_lengths
    placed = jnp.sum(ordered_hot * order_starts[:, :, None], axis=1)
    token_positions = (
        jnp.sum(passage_hot[None, :, :] * placed[:, None, :], axis=2) + offsets[None, :]
    )
    passage_values = raw_value.astype(jnp.bfloat16).reshape(row_count, kv_heads, HEAD_SIZE)
    unrotated_key = unrotated_key.reshape(row_count, kv_heads, HEAD_SIZE)
    scale = HEAD_SIZE ** (-0.5)
    tail_scores = (
        jnp.einsum(
            "tkgd,skd->tkgs", query_vectors, tail_key_rows, preferred_element_type=jnp.float32
        )
        * scale
    )
    causal = jnp.arange(tail_count)[None, :] <= jnp.arange(tail_count)[:, None]
    tail_scores = jnp.where(causal[:, None, None, :], tail_scores, -1e30)
    tail_top = jnp.max(tail_scores, axis=-1)

    def scores_for(places):
        keys = rotate(unrotated_key, places).astype(jnp.bfloat16)
        return (
            jnp.einsum("tkgd,nkd->tkgn", query_vectors, keys, preferred_element_type=jnp.float32)
            * scale
        )

    def local_stats(places):
        scores = scores_for(places)
        peak = jnp.maximum(jnp.max(scores, axis=-1), tail_top)
        return (peak, jnp.sum(jnp.exp(scores - peak[..., None]), axis=-1))

    def combine(first, second):
        peak = jnp.maximum(first[0], second[0])
        return (peak, first[1] * jnp.exp(first[0] - peak) + second[1] * jnp.exp(second[0] - peak))

    peaks, totals = joined(lax.map(local_stats, token_positions), "psg", combine)

    def accumulate(running, inputs):
        places, peak, partial_value = inputs
        weights = jnp.exp(scores_for(places) - peak[..., None])
        tail_weights = jnp.exp(tail_scores - peak[..., None])
        denom = (partial_value + jnp.sum(tail_weights, axis=-1))[..., None]
        shared = jnp.einsum(
            "tkgn,nkd->tkgd",
            weights.astype(jnp.bfloat16),
            passage_values,
            preferred_element_type=jnp.float32,
        )
        own = jnp.einsum(
            "tkgs,skd->tkgd",
            tail_weights.astype(jnp.bfloat16),
            tail_value_rows,
            preferred_element_type=jnp.float32,
        )
        return ((running[0] + shared / denom, running[1] + own / denom), None)

    start_sums = jnp.zeros((tail_count, kv_heads, query_group, HEAD_SIZE), jnp.float32)
    (shared_sum, own_sum), unused_slot = lax.scan(
        accumulate, (start_sums, start_sums), (token_positions, peaks, totals)
    )
    agreed_output = lax.psum(shared_sum, "psg") + own_sum
    mixed = agreed_output.reshape(tail_count, -1).astype(jnp.bfloat16)
    projected = jnp.dot(mixed, w_out, preferred_element_type=jnp.float32)
    squares = lax.psum(jnp.sum(projected * projected, axis=1), "psg")
    factor = lax.rsqrt(squares / MODEL_WIDTH + epsilon)[:, None]
    return (projected * factor * norm_gain[None, :]).astype(jnp.bfloat16)


def solution(mesh):
    placed = (
        P("groups", "psg"),
        P(("groups", "psg"), None),
        P("groups"),
        P("groups"),
        P("groups", None),
        P("psg", None),
        P("psg", None),
        P("psg", None),
        P(None, "psg"),
        P("psg"),
    )
    return jax.shard_map(
        per_device, mesh=mesh, in_specs=placed, out_specs=P("groups", "psg"), check_vma=False
    )
```

profile of v0, /device:TPU:0, one launch (start us, length us, event | category | flops | bytes accessed | tf_op | source)
XLA Modules:
  0.0 504.3 jit_solution(18444703325682669474)
XLA Ops:
  6.5 1.4 convolution_bitcast_fusion.1
  8.0 0.7 copy.70
  8.7 3.0 convolution_bitcast_fusion
  11.7 1.7 copy.65
  13.5 0.7 all-gather.5.cloned.1.call-update
  14.2 0.7 all-gather.7.cloned.1.call-update
  16.1 0.3 fusion.35
  16.5 66.9 %all-reduce.8 = bf16[128,512]{1,0:T(8,128)(2,1)S(1)} all-reduce(f32[128,512]{1,0:T(8,128)S(1)} %fusion.42), channel_id=1, replica_groups=mesh['groups'=2,'psg'=16] {'psg'}, use_global_device_ids=true, to_apply=%region_17.18 | all-reduce | flops 65536 | bytes 393216 | tf_op jit(solution)/shard_map/psum | solution.py:61
  83.4 0.3 multiply_cosine_fusion.2
  83.7 0.7 copy_bitcast_fusion.1
  84.4 31.9 %all-reduce.7.cloned.1.call-done = (f32[128,32,128]{2,1,0:T(8,128)}, f32[128,4,128]{2,0,1:T(8,128)}) async-done(((f32[128,32,128]{2,1,0:T(8,128)}, f32[128,4,128]{2,0,1:T(8,128)}), (f32[128,32,128]{2,1,0:T(8,128)}, f32[128,4,128]{2,0,1:T(8,128)})) %all-reduce.7.cloned.1.call-update) | async-done | bytes 2359312 | tf_op jit(solution)/shard_map/psum | solution.py:61
  116.3 3.0 subtract_convert_fusion.2
  119.3 0.4 copy.46
  119.7 0.4 copy.47
  120.2 0.6 pad_maximum_fusion
  120.8 0.3 copy-done.7
  121.2 1.8 fusion.41
  123.1 1.9 copy.52
  125.0 67.9 %all-gather.5.cloned.1.call-done = bf16[8192,512]{1,0:T(8,128)(2,1)} async-done(((bf16[512,512]{1,0:T(8,128)(2,1)}), bf16[8192,512]{1,0:T(8,128)(2,1)}) %all-gather.5.cloned.1.call-update) | async-done | bytes 8388624 | tf_op jit(solution)/shard_map/all_gather | solution.py:75
  192.9 4.9 convolution_bitcast_fusion.2
  197.8 70.4 %all-gather.7.cloned.1.call-done = bf16[8192,512]{1,0:T(8,128)(2,1)} async-done(((bf16[512,512]{1,0:T(8,128)(2,1)}), bf16[8192,512]{1,0:T(8,128)(2,1)}) %all-gather.7.cloned.1.call-update) | async-done | bytes 8388624 | tf_op jit(solution)/shard_map/all_gather | solution.py:76
  268.2 4.9 fusion.31
  273.1 0.6 copy.72
  273.8 7.1 %while.46 = (s32[]{:T(128)}, f32[3,128,4,8]{1,3,2,0:T(8,128)S(1)}, f32[3,128,4,8]{1,3,2,0:T(8,128)S(1)}, f32[64,4,128]{2,0,1:T(8,128)S(1)}, s32[3,64]{1,0:T(4,12...) while((s32[]{:T(128)}, f32[3,128,4,8]{1,3,2,0:T(8,128)S(1)}, ...), condition=%wide.region_14.15_spmd, body=%wide.region_11.14_spmd.sunk | while | flops 68419776 | bytes 3622249 | solution.py:123
  274.1 1.8 fusion.73
  276.5 1.8 fusion.73
  278.9 1.8 fusion.73
  280.9 20.9 %all-gather.1 = f32[48,128,4,8]{1,3,2,0:T(8,128)S(1)} all-gather(f32[3,128,4,8]{1,3,2,0:T(8,128)S(1)} %get-tuple-element.367), channel_id=3, replica_groups=mesh['groups'=2,'psg'=16] {'psg'}, dimensions={0}, use_global_device_ids=true | all-gather | bytes 835584 | tf_op jit(solution)/shard_map/all_gather | solution.py:15
  301.7 19.8 %all-gather = f32[48,128,4,8]{1,3,2,0:T(8,128)S(1)} all-gather(f32[3,128,4,8]{1,3,2,0:T(8,128)S(1)} %get-tuple-element.366), channel_id=2, replica_groups=mesh['groups'=2,'psg'=16] {'psg'}, dimensions={0}, use_global_device_ids=true | all-gather | bytes 835584 | tf_op jit(solution)/shard_map/all_gather | solution.py:15
  321.6 0.9 copy-done.5
  322.4 13.5 %while.47 = (s32[]{:T(128)}, f32[3,128,4,8]{1,3,2,0:T(8,128)S(1)}, f32[3,128,4,8]{1,3,2,0:T(8,128)S(1)}, f32[16,3,128,4,8]{2,4,3,1,0:T(8,128)}, f32[16,3,128,4,8...) while((s32[]{:T(128)}, f32[3,128,4,8]{1,3,2,0:T(8,128)S(1)}, f32[3,128,4,8]{1,3,2,0:T(8,128)S(1)}, ...), condition=%wide.region_16.17_spmd, body=%wide.region_15.16_spmd.sunk | while | flops 73733 | bytes 295035 | solution.py:20
  322.4 0.9 fusion.74
  323.3 0.9 fusion.74
  324.2 0.9 fusion.74
  325.1 0.9 fusion.74
  326.0 0.9 fusion.74
  326.9 0.9 fusion.74
  327.8 0.9 fusion.74
  328.7 0.9 fusion.74
  329.6 0.9 fusion.74
  330.5 0.9 fusion.74
  331.4 0.9 fusion.74
  332.3 0.9 fusion.74
  333.2 0.9 fusion.74
  334.1 0.9 fusion.74
  335.0 0.9 fusion.74
  335.9 27.7 %while.48 = (s32[]{:T(128)}, f32[128,4,8,128]{3,0,2,1:T(8,128)}, f32[128,4,8,128]{3,0,2,1:T(8,128)}, f32[64,4,128]{2,0,1:T(8,128)S(1)}, s32[3,64]{1,0:T(4,128)S(...) while((s32[]{:T(128)}, f32[128,4,8,128]{3,0,2,1:T(8,128)}, ...), condition=%wide.region_20.21_spmd.clone, body=%wide.region_18.20_spmd.clone.sunk | while | flops 274731200 | bytes 14337436 | solution.py:145
  336.0 1.3 fusion.79
  337.6 3.7 fusion.81
  341.3 3.2 fusion.82
  344.5 1.3 fusion.79
  346.1 4.4 fusion.81
  350.5 3.5 fusion.82
  354.1 1.3 fusion.79
  355.7 4.4 fusion.81
  360.1 3.5 fusion.82
  363.6 2.9 copy.54
  366.6 1.9 copy.55
  368.5 94.4 %all-reduce.5.cloned.1.call-done = f32[128,4,8,128]{0,3,2,1:T(8,128)} async-done(((f32[128,4,8,128]{0,3,2,1:T(8,128)}), f32[128,4,8,128]{0,3,2,1:T(8,128)}) %all-reduce.5.cloned.1.call-update) | async-done | bytes 2097168 | tf_op jit(solution)/shard_map/psum | solution.py:148
  462.9 2.0 add_convert_fusion.2
  465.0 0.8 copy-done.2
  465.7 0.8 multiply_reduce_fusion
  466.6 30.4 %psum.39 = f32[128]{0:T(128)S(1)} all-reduce(f32[128]{0:T(128)S(1)} %get-tuple-element.550), channel_id=1, replica_groups=mesh['groups'=2,'psg'=16] {'psg'}, use_global_device_ids=true, to_apply=%region_23.24 | all-reduce | flops 128 | bytes 1024 | tf_op jit(solution)/shard_map/psum | solution.py:151
  497.0 0.8 multiply_convert_fusion
  (93 shorter events, 4.1 us)
Async XLA Ops:
  6.5 186.3 %copy-start = (bf16[64,8192]{1,0:T(8,128)(2,1)S(1)}, bf16[64,8192]{1,0:T(8,128)(2,1)}, u32[]{:S(2)}) copy-start(bf16[64,8192]{1,0:T(8,128)(2,1)} %param.17) | copy-start | bytes 3145732
  6.5 109.8 %all-reduce.7.cloned.1.call-start = ((), (), s32[]{:S(2)}) async-start(), calls=%async_computation.3 | async-start | bytes 4718592 | tf_op jit(solution)/shard_map/psum | solution.py:61
  13.4 1.6 copy-start.10
  13.4 1.6 copy-start.11
  13.4 2.0 copy-start.8
  13.4 2.2 copy-start.3
  13.4 2.2 copy-start.6
  13.4 179.4 %all-gather.5.cloned.1.call-start = ((), (), s32[]{:S(2)}) async-start(), calls=%async_computation | async-start | bytes 8912896 | tf_op jit(solution)/shard_map/all_gather | solution.py:75
  14.2 254.0 %all-gather.7.cloned.1.call-start = ((), (), s32[]{:S(2)}) async-start(), calls=%async_computation.1 | async-start | bytes 8912896 | tf_op jit(solution)/shard_map/all_gather | solution.py:76
  14.9 448.0 %all-reduce.5.cloned.1.call-start = ((), (), s32[]{:S(2)}) async-start(), calls=%async_computation.2 | async-start | bytes 4194304 | tf_op jit(solution)/shard_map/psum | solution.py:148
  120.1 1.0 copy-start.7
  120.8 2.3 copy-start.1
  301.7 19.8 %copy-start.4 = (f32[48,128,4,8]{1,3,2,0:T(8,128)}, f32[48,128,4,8]{1,3,2,0:T(8,128)S(1)}, u32[]{:S(2)}) copy-start(f32[48,128,4,8]{1,3,2,0:T(8,128)S(1)} %all-gather.1) | copy-start | bytes 2359300
  321.6 0.9 copy-start.5
  462.9 2.8 copy-start.2
  465.7 31.2 %copy-start.9 = (f32[512]{0:T(512)S(1)}, f32[512]{0:T(512)}, u32[]{:S(2)}) copy-start(f32[512]{0:T(512)} %param.25) | copy-start | bytes 6148
Sparse Core Ops, SparseCore 0:
  13.6 102.6 all-reduce.6
  118.5 74.3 all-gather.4
  195.0 73.1 all-gather.6
  366.7 96.1 all-reduce.4
where the time goes:
time: 506 us; the launch traced here: 504 us
  waiting for transfers between devices  266 us (53%)
  blocking collectives  138 us (27%)
  matrix products  45.3 us (9%)
  other arithmetic  27.3 us (5%)
  local copies, waits for them, and re-layouts  13.5 us (3%)
  between operations  13.4 us (3%)
    psum x1, waiting for transfers between devices, per_device(): agreed_output = lax.psum(shared_sum, 'psg') + own_sum  94.4 us
    all_gather x1, waiting for transfers between devices, per_device(): lax.all_gather(value_weight, 'psg', axis=0, tiled=True)  70.4 us
    all_gather x1, waiting for transfers between devices, per_device(): lax.all_gather(key_weight, 'psg', axis=0, tiled=True)  67.9 us
    psum x1, blocking collectives, per_device(): lax.psum((query_part, key_part, value_part), 'psg')  66.9 us
    all_gather x2, blocking collectives, joined(): gathered = jax.tree.map(lambda a: lax.all_gather(a, axis), part)  40.7 us
    psum x1, waiting for transfers between devices, per_device(): lax.psum((query_part, key_part, value_part), 'psg')  31.9 us
    psum x1, blocking collectives, per_device(): squares = lax.psum(jnp.sum(projected * projected, axis=1), 'psg')  30.4 us
    add x15, other arithmetic, combine(): first[1] * jnp.exp(first[0] - peak) + second[1] * jnp.exp(second[0] - peak)  13.2 us
  transfers between devices with their start and end apart: 4, of which 4 were waited for; matrix products, arithmetic and copies ran while one was open for 3% of the time, Pallas kernels for 0%

commit v1 on v0

--- a/solution.py
+++ b/solution.py
@@ -35,7 +35,130 @@
     )
 
 
-def per_device(
+def running_sum(values):
+    count = values.shape[-1]
+    earlier = (jnp.arange(count)[None, :] <= jnp.arange(count)[:, None]).astype(values.dtype)
+    return jnp.sum(earlier * values[..., None, :], axis=-1)
+
+
+def token_places(lengths, storage_order, orders, row_ids):
+    numbers = jnp.arange(lengths.shape[0], dtype=jnp.int32)
+    pick = (storage_order[:, None] == numbers[None, :]).astype(jnp.int32)
+    stored_lengths = jnp.sum(pick * lengths[None, :], axis=1)
+    ends = running_sum(stored_lengths)
+    starts = ends - stored_lengths
+    slots = jnp.sum((ends[None, :] <= row_ids[:, None]).astype(jnp.int32), axis=1)
+    in_slot = (slots[:, None] == numbers[None, :]).astype(jnp.int32)
+    offsets = row_ids - jnp.sum(in_slot * starts[None, :], axis=1)
+    passage_hot = jnp.sum(in_slot[:, :, None] * pick[None, :, :], axis=1)
+    ordered_hot = (orders[:, :, None] == numbers[None, None, :]).astype(jnp.int32)
+    ordered_lengths = jnp.sum(ordered_hot * lengths[None, None, :], axis=2)
+    order_starts = running_sum(ordered_lengths) - ordered_lengths
+    placed = jnp.sum(ordered_hot * order_starts[:, :, None], axis=1)
+    return jnp.sum(passage_hot[None, :, :] * placed[:, None, :], axis=2) + offsets[None, :]
+
+
+def by_heads(
+    tail_hidden_states,
+    passage_hidden_states,
+    lengths,
+    storage_order,
+    orders,
+    w_query,
+    key_weight,
+    value_weight,
+    w_out,
+    norm_gain,
+):
+    shards = lax.axis_size("psg")
+    device = lax.axis_index("psg")
+    row_count, width = passage_hidden_states.shape
+    tail_count, depth = tail_hidden_states.shape
+    kv_heads = key_weight.shape[1] // HEAD_SIZE
+    own_heads = w_query.shape[1] // HEAD_SIZE // shards
+    share = shards // kv_heads
+    total_keys = row_count * shards
+    rows = total_keys // share
+    tail_rows = tail_count // share
+    perms = orders.shape[0]
+    place = device % share
+
+    query_part = jnp.einsum(
+        "td,dsc->stc",
+        tail_hidden_states,
+        w_query.reshape(depth, shards, own_heads * HEAD_SIZE),
+        preferred_element_type=jnp.float32,
+    )
+    query_sum = lax.psum_scatter(query_part, "psg", scatter_dimension=0)
+    slab = lax.all_to_all(passage_hidden_states, "psg", 1, 0, tiled=True)
+    slab = jnp.concatenate(
+        [slab.reshape(share, rows, depth), tail_hidden_states.reshape(share, tail_rows, depth)],
+        axis=1,
+    )
+    both = jnp.concatenate(
+        [
+            key_weight.reshape(depth, kv_heads, HEAD_SIZE),
+            value_weight.reshape(depth, kv_heads, HEAD_SIZE),
+        ],
+        axis=2,
+    )
+    pair_part = jnp.einsum("rnd,dkc->krnc", slab, both, preferred_element_type=jnp.float32)
+    pair_sum = lax.psum_scatter(
+        pair_part.reshape(shards, rows + tail_rows, 2 * HEAD_SIZE), "psg", scatter_dimension=0
+    )
+
+    tail_pos = total_keys + jnp.arange(tail_count, dtype=jnp.int32)
+    query = rotate(query_sum.reshape(tail_count, own_heads, HEAD_SIZE), tail_pos)
+    query = query.astype(jnp.bfloat16)
+    own_rows = place * rows + jnp.arange(rows, dtype=jnp.int32)
+    places = token_places(lengths, storage_order, orders, own_rows)
+    own_tail = total_keys + place * tail_rows + jnp.arange(tail_rows, dtype=jnp.int32)
+    raw_key = pair_sum[:, :HEAD_SIZE]
+    unrotated = jnp.concatenate([raw_key[:rows]] * perms + [raw_key[rows:]])
+    spots = jnp.concatenate([places.reshape(-1), own_tail])
+    own_keys = rotate(unrotated[:, None, :], spots)[:, 0, :].astype(jnp.bfloat16)
+    own_values = pair_sum[:, HEAD_SIZE:].astype(jnp.bfloat16)
+    packed = jnp.concatenate([own_keys, own_values])
+    alike = [[k * share + i for i in range(share)] for k in range(kv_heads)]
+    every = lax.all_gather(packed, "psg", axis_index_groups=alike)
+    cut = perms * rows
+    keys = every[:, :cut].reshape(share, perms, rows, HEAD_SIZE)
+    tail_keys = every[:, cut : cut + tail_rows].reshape(tail_count, HEAD_SIZE)
+    low = cut + tail_rows
+    values = every[:, low : low + rows].reshape(total_keys, HEAD_SIZE)
+    tail_values = every[:, low + rows :].reshape(tail_count, HEAD_SIZE)
+
+    scale = HEAD_SIZE ** (-0.5)
+    scores = (
+        jnp.einsum("tgd,spnd->ptgsn", query, keys, preferred_element_type=jnp.float32) * scale
+    ).reshape(perms, tail_count, own_heads, total_keys)
+    tail_scores = (
+        jnp.einsum("tgd,sd->tgs", query, tail_keys, preferred_element_type=jnp.float32) * scale
+    )
+    causal = jnp.arange(tail_count)[None, :] <= jnp.arange(tail_count)[:, None]
+    tail_scores = jnp.where(causal[:, None, :], tail_scores, -1e30)
+    peak = jnp.maximum(jnp.max(scores, axis=-1), jnp.max(tail_scores, axis=-1))[..., None]
+    weights = jnp.exp(scores - peak)
+    tail_weights = jnp.exp(tail_scores - peak)
+    denom = jnp.sum(weights, axis=-1) + jnp.sum(tail_weights, axis=-1)
+    numer = jnp.einsum(
+        "ptgn,nd->ptgd", weights.astype(jnp.bfloat16), values, preferred_element_type=jnp.float32
+    ) + jnp.einsum(
+        "ptgs,sd->ptgd",
+        tail_weights.astype(jnp.bfloat16),
+        tail_values,
+        preferred_element_type=jnp.float32,
+    )
+    agreed = jnp.sum(numer / denom[..., None], axis=0)
+    own_mixed = agreed.reshape(tail_count, own_heads * HEAD_SIZE).astype(jnp.bfloat16)
+    mixed = lax.all_gather(own_mixed, "psg", axis=1, tiled=True)
+    projected = jnp.dot(mixed, w_out, preferred_element_type=jnp.float32)
+    squares = lax.psum(jnp.sum(projected * projected, axis=1), "psg")
+    factor = lax.rsqrt(squares / width + epsilon)[:, None]
+    return (projected * factor * norm_gain[None, :]).astype(jnp.bfloat16)
+
+
+def by_rows(
     tail_hidden_states,
     passage_hidden_states,
     lengths,
@@ -74,23 +197,8 @@
 
     unrotated_key = add_block(lax.all_gather(key_weight, "psg", axis=0, tiled=True))
     raw_value = add_block(lax.all_gather(value_weight, "psg", axis=0, tiled=True))
-    numbers = jnp.arange(lengths.shape[0], dtype=jnp.int32)
-    pick = (storage_order[:, None] == numbers[None, :]).astype(jnp.int32)
-    stored_lengths = jnp.sum(pick * lengths[None, :], axis=1)
-    ends = jnp.cumsum(stored_lengths)
-    starts = ends - stored_lengths
     row_ids = device * row_count + jnp.arange(row_count, dtype=jnp.int32)
-    slots = jnp.sum((ends[None, :] <= row_ids[:, None]).astype(jnp.int32), axis=1)
-    in_slot = (slots[:, None] == numbers[None, :]).astype(jnp.int32)
-    offsets = row_ids - jnp.sum(in_slot * starts[None, :], axis=1)
-    passage_hot = jnp.dot(in_slot, pick)
-    ordered_hot = (orders[:, :, None] == numbers[None, None, :]).astype(jnp.int32)
-    ordered_lengths = jnp.sum(ordered_hot * lengths[None, None, :], axis=2)
-    order_starts = jnp.cumsum(ordered_lengths, axis=1) - ordered_lengths
-    placed = jnp.sum(ordered_hot * order_starts[:, :, None], axis=1)
-    token_positions = (
-        jnp.sum(passage_hot[None, :, :] * placed[:, None, :], axis=2) + offsets[None, :]
-    )
+    token_positions = token_places(lengths, storage_order, orders, row_ids)
     passage_values = raw_value.astype(jnp.bfloat16).reshape(row_count, kv_heads, HEAD_SIZE)
     unrotated_key = unrotated_key.reshape(row_count, kv_heads, HEAD_SIZE)
     scale = HEAD_SIZE ** (-0.5)
@@ -151,6 +259,17 @@
     squares = lax.psum(jnp.sum(projected * projected, axis=1), "psg")
     factor = lax.rsqrt(squares / MODEL_WIDTH + epsilon)[:, None]
     return (projected * factor * norm_gain[None, :]).astype(jnp.bfloat16)
+
+
+def per_device(*arrays):
+    tail_hidden_states, w_query, key_weight = arrays[0], arrays[5], arrays[6]
+    shards = lax.axis_size("psg")
+    query_heads = w_query.shape[1] // HEAD_SIZE
+    kv_heads = key_weight.shape[1] // HEAD_SIZE
+    fits = query_heads % shards == 0 and shards % kv_heads == 0
+    if fits and tail_hidden_states.shape[0] % (shards // kv_heads) == 0:
+        return by_heads(*arrays)
+    return by_rows(*arrays)
 
 
 def solution(mesh):

time: 506 us -> 307 us (0.61)
  blocking collectives: 138 us -> 31.6 us
  waiting for transfers between devices: 266 us -> 211 us
  matrix products: 45.3 us -> 14.8 us
  other arithmetic: 27.3 us -> 4.05 us
  local copies, waits for them, and re-layouts: 13.5 us -> 23.9 us
  starting transfers between devices: 0.12 us -> 7.66 us
    reduce_scatter x0 -> x2, waiting for transfers between devices: none -> 134 us  [the longest x1 74.7 us: by_heads(): lax.psum_scatter(pair_part.reshape(shards, rows + tail_rows, 2 * HEAD_SIZ...]
    psum x2 -> x0, waiting for transfers between devices: 126 us -> none  [the longest x1 94.4 us: per_device(): agreed_output = lax.psum(shared_sum, 'psg') + own_sum]
    all_gather x2, waiting for transfers between devices: 138 us -> 54.7 us  [the longest x1 38.1 us: by_heads(): mixed = lax.all_gather(own_mixed, 'psg', axis=1, tiled=True)]
    psum x2 -> x1, blocking collectives: 97.3 us -> 31.6 us  [by_heads(): squares = lax.psum(jnp.sum(projected * projected, axis=1), 'psg')]
    all_gather x2 -> x0, blocking collectives: 40.7 us -> none  [joined(): gathered = jax.tree.map(lambda a: lax.all_gather(a, axis), part)]
    dot_general x17 -> x7, matrix products: 45.3 us -> 14.8 us  [the longest x1 5.04 us: by_heads(): jnp.einsum('td,dsc->stc', tail_hidden_states, w_query.reshape(depth, shar...]
    all_to_all x0 -> x1, waiting for transfers between devices: none -> 21.9 us  [by_heads(): slab = lax.all_to_all(passage_hidden_states, 'psg', 1, 0, tiled=True)]
    add x20 -> x4, other arithmetic: 13.2 us -> 0.02 us  [the longest x1 0.01 us: by_heads(): own_rows = place * rows + jnp.arange(rows, dtype=jnp.int32)]
  transfers between devices with their start and end apart: 4 -> 5, of which waited for: 4 -> 5; matrix products, arithmetic and copies ran while one was open for 3% -> 6% of each run, Pallas kernels for 0% -> 0%
where the time goes in v1:
time: 307 us; the launch traced here: 306 us
  waiting for transfers between devices  211 us (69%)
  blocking collectives  31.6 us (10%)
  local copies, waits for them, and re-layouts  23.9 us (8%)
  matrix products  14.8 us (5%)
  between operations  13.4 us (4%)
  starting transfers between devices  7.66 us (2%)
  other arithmetic  4.05 us (1%)
    reduce_scatter x1, waiting for transfers between devices, by_heads(): lax.psum_scatter(pair_part.reshape(shards, rows + tail_rows, 2 * HEAD_SIZ...  74.7 us
    reduce_scatter x1, waiting for transfers between devices, by_heads(): query_sum = lax.psum_scatter(query_part, 'psg', scatter_dimension=0)  59.7 us
    all_gather x1, waiting for transfers between devices, by_heads(): mixed = lax.all_gather(own_mixed, 'psg', axis=1, tiled=True)  38.1 us
    psum x1, blocking collectives, by_heads(): squares = lax.psum(jnp.sum(projected * projected, axis=1), 'psg')  31.6 us
    all_to_all x1, waiting for transfers between devices, by_heads(): slab = lax.all_to_all(passage_hidden_states, 'psg', 1, 0, tiled=True)  21.9 us
    all_gather x1, waiting for transfers between devices, by_heads(): every = lax.all_gather(packed, 'psg', axis_index_groups=alike)  16.6 us
    all_to_all x1, starting transfers between devices, by_heads(): slab = lax.all_to_all(passage_hidden_states, 'psg', 1, 0, tiled=True)  7.49 us
    reshape x1, local copies, waits for them, and re-layouts, by_heads(): w_query.reshape(depth, shards, own_heads * HEAD_SIZE)  6.58 us
  transfers between devices with their start and end apart: 5, of which 5 were waited for; matrix products, arithmetic and copies ran while one was open for 6% of the time, Pallas kernels for 0%

profile of v1, /device:TPU:0, one launch (start us, length us, event | category | flops | bytes accessed | tf_op | source)
XLA Modules:
  0.0 306.4 jit_solution(701727399858984622)
XLA Ops:
  6.5 2.4 copy.148
  9.0 7.5 %all-to-all-start = ((bf16[64,16,512]{2,0,1:T(8,128)(2,1)}), bf16[64,16,512]{2,0,1:T(8,128)(2,1)S(1)}, u32[]{:S(2)}, u32[]{:S(2)}) async-start(bf16[64,16,512]{2,0,1:T(8,128)(2,1)} %bitcast.75), calls=%async_computation | async-start | bytes 2097152 | tf_op jit(solution)/shard_map/all_to_all | solution.py:93
  16.5 0.0 reduce-scatter.3.cloned.1.call-start
  16.5 0.0 copy-done.1
  16.5 0.2 copy.115
  16.7 0.3 copy.117
  17.0 0.0 copy-done.2
  17.0 0.2 copy.114
  17.2 0.3 copy.116
  17.5 21.9 %all-to-all-done = bf16[64,16,512]{2,0,1:T(8,128)(2,1)S(1)} async-done(((bf16[64,16,512]{2,0,1:T(8,128)(2,1)}), bf16[64,16,512]{2,0,1:T(8,128)(2,1)S(1)}, u32[]{:S(2)}, u32[]{:S(2)}) %all-to-all-start) | async-done | bytes 1048608 | tf_op jit(solution)/shard_map/all_to_all | solution.py:93
  39.4 0.0 copy-done
  39.4 3.6 %convolution_bitcast_fusion = f32[4,4,288,256]{3,2,1,0:T(8,128)} fusion(bf16[4,32,512]{2,1,0:T(8,128)(2,1)S(1)} %bitcast.86, bf16[4,256,512]{2,1,0:T(8,128)(2,1)S(1)} %bitcast.78, bf16[512,4,128]{2,0,1:T(8,128)(2,1)S(1)} %copy.117, bf16[512,4,128]{2,0,1:T(8,128)(2,1)S(1)} %copy.116), kind=kOutput, calls=%fused_computation.5 | convolution fusion | flops 1212416000 | bytes 6946816 | tf_op jit(solution)/shard_map/rnd,dkc->krnc/dot_general | solution.py:105
  43.0 6.2 %copy.119 = f32[4,4,288,256]{2,3,1,0:T(8,128)} copy(f32[4,4,288,256]{3,2,1,0:T(8,128)} %convolution_bitcast_fusion) | data formatting | bytes 9437184 | tf_op jit(solution)/shard_map/rnd,dkc->krnc/transpose | solution.py:105
  49.2 0.0 reduce-scatter.3.cloned.1.call-update
  49.3 0.0 reduce-scatter.5.cloned.1.call-start
  49.3 6.6 %copy.139 = bf16[512,4096]{0,1:T(8,128)(2,1)} copy(bf16[512,4096]{1,0:T(8,128)(2,1)} %param.15) | data formatting | bytes 8388608 | tf_op jit(solution)/shard_map/reshape | solution.py:89
  55.9 5.0 %convolution_bitcast_fusion.1 = f32[16,128,256]{1,2,0:T(8,128)} fusion(bf16[512,16,256]{0,2,1:T(8,128)(2,1)} %bitcast.77, bf16[128,512]{1,0:T(8,128)(2,1)S(1)} %copy-done), kind=kOutput, calls=%fused_computation.6 | convolution fusion | flops 536870912 | bytes 6422528 | tf_op jit(solution)/shard_map/td,dsc->stc/dot_general | solution.py:86
  60.9 0.0 reduce-scatter.5.cloned.1.call-update
  61.0 0.0 all-gather.6.cloned.1.call-start
  61.0 0.0 copy-done.3
  61.0 0.0 copy-done.5
  61.1 0.1 select_reduce_fusion.2
  61.1 0.1 multiply_reduce_fusion.3
  61.3 0.1 copy.120
  61.4 0.0 copy-done.6
  61.4 0.2 select_reduce_fusion.4
  61.5 0.1 select_reduce_fusion.3
  61.7 0.1 fusion.28
  61.8 0.1 select_reduce_fusion
  61.9 0.1 fusion.30
  61.9 0.1 multiply_reduce_fusion.2
  62.0 0.1 multiply_reduce_fusion.1
  62.2 74.7 %reduce-scatter.3.cloned.1.call-done = f32[1,288,256]{1,2,0:T(8,128)} async-done(((f32[16,288,256]{1,2,0:T(8,128)}), f32[1,288,256]{1,2,0:T(8,128)}) %reduce-scatter.3.cloned.1.call-update) | async-done | bytes 294928 | tf_op jit(solution)/shard_map/reduce_scatter | solution.py:106
  136.9 0.9 slice.67
  137.8 0.9 slice.50
  138.8 0.9 slice.49
  139.7 0.9 fusion.21
  140.7 0.1 pad_maximum_fusion
  140.8 0.9 copy.121
  141.7 0.0 all-gather.6.cloned.1.call-update
  141.7 0.0 all-gather.4.cloned.1.call-start
  141.8 0.3 multiply_cosine_fusion.1
  142.1 59.7 %reduce-scatter.5.cloned.1.call-done = f32[1,128,256]{1,2,0:T(8,128)} async-done(((f32[16,128,256]{1,2,0:T(8,128)}), f32[1,128,256]{1,2,0:T(8,128)}) %reduce-scatter.5.cloned.1.call-update) | async-done | bytes 131088 | tf_op jit(solution)/shard_map/reduce_scatter | solution.py:92
  201.8 0.9 fusion.38
  202.7 0.1 copy.142
  202.8 0.1 copy.141
  202.9 16.6 %all-gather.6.cloned.1.call-done = bf16[4352,128]{1,0:T(8,128)(2,1)} async-done(((bf16[1088,128]{1,0:T(8,128)(2,1)}), bf16[4352,128]{1,0:T(8,128)(2,1)}) %all-gather.6.cloned.1.call-update) | async-done | bytes 1114128 | tf_op jit(solution)/shard_map/all_gather | solution.py:123
  219.5 0.8 fusion.37
  220.3 1.2 slice.54
  221.5 0.7 bitcast_reduce_fusion
  222.2 0.3 fusion.39
  222.5 1.6 fusion.3
  224.1 0.5 fusion.1
  224.6 0.1 copy.126
  224.7 0.3 fusion.14
  225.1 0.2 fusion.10
  225.3 0.0 copy-start.4
  225.3 0.7 copy.130
  226.0 0.0 all-gather.4.cloned.1.call-update
  226.1 38.1 %all-gather.4.cloned.1.call-done = bf16[128,4096]{0,1:T(8,128)(2,1)} async-done(((bf16[128,256]{0,1:T(8,128)(2,1)}), bf16[128,4096]{0,1:T(8,128)(2,1)}) %all-gather.4.cloned.1.call-update) | async-done | bytes 1048592 | tf_op jit(solution)/shard_map/all_gather | solution.py:154
  264.2 3.3 %multiply_reduce_fusion = (f32[128]{0:T(128)S(1)}, f32[128,512]{1,0:T(8,128)S(1)}) fusion(bf16[128,4096]{0,1:T(8,128)(2,1)} %all-gather.4.cloned.1.call-done, bf16[4096,512]{1,0:T(8,128)(2,1)} %param.18), kind=kOutput, calls=%fused_computation.35 | convolution fusion | flops 537001856 | bytes 5505536 | tf_op jit(solution)/shard_map/dot_general | solution.py:155
  267.5 31.6 %psum.7 = f32[128]{0:T(128)S(1)} all-reduce(f32[128]{0:T(128)S(1)} %get-tuple-element.21), channel_id=1, replica_groups=mesh['groups'=2,'psg'=16] {'psg'}, use_global_device_ids=true, to_apply=%region_17.18 | all-reduce | flops 128 | bytes 1024 | tf_op jit(solution)/shard_map/psum | solution.py:156
  299.1 0.0 copy-done.4
  299.1 0.8 multiply_convert_fusion
  (27 shorter events, 0.2 us)
Async XLA Ops:
  6.5 10.0 %copy-start.1 = (bf16[512,512]{1,0:T(8,128)(2,1)S(1)}, bf16[512,512]{1,0:T(8,128)(2,1)}, u32[]{:S(2)}) copy-start(bf16[512,512]{1,0:T(8,128)(2,1)} %param.17) | copy-start | bytes 1572868
  6.5 10.5 %copy-start.2 = (bf16[512,512]{1,0:T(8,128)(2,1)S(1)}, bf16[512,512]{1,0:T(8,128)(2,1)}, u32[]{:S(2)}) copy-start(bf16[512,512]{1,0:T(8,128)(2,1)} %param.16) | copy-start | bytes 1572868
  9.0 30.4 %copy-start = (bf16[128,512]{1,0:T(8,128)(2,1)S(1)}, bf16[128,512]{1,0:T(8,128)(2,1)}, u32[]{:S(2)}) copy-start(bf16[128,512]{1,0:T(8,128)(2,1)} %param.10) | copy-start | bytes 393220
  9.0 30.4 %all-to-all-start = ((bf16[64,16,512]{2,0,1:T(8,128)(2,1)}), bf16[64,16,512]{2,0,1:T(8,128)(2,1)S(1)}, u32[]{:S(2)}, u32[]{:S(2)}) async-start(bf16[64,16,512]{2,0,1:T(8,128)(2,1)} %bitcast.75), calls=%async_computation | async-start | bytes 2097152 | tf_op jit(solution)/shard_map/all_to_all | solution.py:93
  16.5 120.4 %reduce-scatter.3.cloned.1.call-start = ((), (), s32[]{:S(2)}) async-start(), calls=%async_computation.3 | async-start | bytes 6684672 | tf_op jit(solution)/shard_map/reduce_scatter | solution.py:106
  49.3 152.5 %reduce-scatter.5.cloned.1.call-start = ((), (), s32[]{:S(2)}) async-start(), calls=%async_computation.4 | async-start | bytes 2228224 | tf_op jit(solution)/shard_map/reduce_scatter | solution.py:92
  55.9 5.1 %copy-start.3 = (s32[3,2]{0,1:T(2,128)S(1)}, s32[3,2]{0,1:T(2,128)}, u32[]{:S(2)}) copy-start(s32[3,2]{0,1:T(2,128)} %param.14) | copy-start | bytes 76
  55.9 5.2 %copy-start.5 = (s32[2]{0:T(128)S(1)}, s32[2]{0:T(128)}, u32[]{:S(2)}) copy-start(s32[2]{0:T(128)} %param.12) | copy-start | bytes 28
  55.9 5.5 %copy-start.6 = (s32[2]{0:T(128)S(1)}, s32[2]{0:T(128)}, u32[]{:S(2)}) copy-start(s32[2]{0:T(128)} %param.13) | copy-start | bytes 28
  61.0 158.5 %all-gather.6.cloned.1.call-start = ((), (), s32[]{:S(2)}) async-start(), calls=%async_computation.6 | async-start | bytes 1392640 | tf_op jit(solution)/shard_map/all_gather | solution.py:123
  141.7 122.5 %all-gather.4.cloned.1.call-start = ((), (), s32[]{:S(2)}) async-start(), calls=%async_computation.5 | async-start | bytes 1114112 | tf_op jit(solution)/shard_map/all_gather | solution.py:154
  225.3 73.8 %copy-start.4 = (f32[512]{0:T(512)S(1)}, f32[512]{0:T(512)}, u32[]{:S(2)}) copy-start(f32[512]{0:T(512)} %param.19) | copy-start | bytes 6148
Sparse Core Ops, SparseCore 0:
  49.4 87.4 reduce-scatter.2
  141.1 60.6 reduce-scatter.4
  203.3 16.1 all-gather.5
  226.2 37.9 all-gather.3

commit v2 on v1

--- a/solution.py
+++ b/solution.py
@@ -1,6 +1,10 @@
+import functools
+
 import jax
 import jax.numpy as jnp
 from jax import lax
+from jax.experimental import pallas as pl
+from jax.experimental.pallas import tpu as pltpu
 from jax.sharding import PartitionSpec as P
 
 MODEL_WIDTH = 8192
@@ -56,6 +60,114 @@
     order_starts = running_sum(ordered_lengths) - ordered_lengths
     placed = jnp.sum(ordered_hot * order_starts[:, :, None], axis=1)
     return jnp.sum(passage_hot[None, :, :] * placed[:, None, :], axis=2) + offsets[None, :]
+
+
+def backwards(index, bits):
+    return sum((index // 2**b) % 2 * 2 ** (bits - 1 - b) for b in range(bits))
+
+
+def closing_kernel(
+    bits, width, own_ref, w_ref, gain_ref, out_ref, held, total, given, got, sends, lands
+):
+    me = lax.axis_index("psg")
+    partners = [me + (1 - 2 * ((me // 2**b) % 2)) * 2**b for b in reversed(range(bits))]
+    barrier = pltpu.get_barrier_semaphore()
+    for partner in partners:
+        pl.semaphore_signal(
+            barrier, inc=1, device_id={"psg": partner}, device_id_type=pl.DeviceIdType.MESH
+        )
+    pl.semaphore_wait(barrier, bits)
+
+    slot = backwards(me, bits)
+    held[slot] = own_ref[...]
+    for step, partner in enumerate(partners):
+        run = pl.ds(slot // 2**step * 2**step, 2**step)
+        copy = pltpu.make_async_remote_copy(
+            src_ref=held.at[run],
+            dst_ref=held.at[run],
+            send_sem=sends.at[step],
+            recv_sem=lands.at[step],
+            device_id={"psg": partner},
+            device_id_type=pl.DeviceIdType.MESH,
+        )
+        copy.start()
+        copy.wait()
+    part = own_ref.shape[1]
+    for j in range(2**bits):
+        product = jnp.dot(
+            held[backwards(j, bits)],
+            w_ref[j * part : (j + 1) * part, :],
+            preferred_element_type=jnp.float32,
+        )
+        if j == 0:
+            total[...] = product
+        else:
+            total[...] += product
+
+    projected = total[...]
+    squared = projected * projected
+    folded = sum(squared[:, c : c + 128] for c in range(0, squared.shape[1], 128))
+    sums = jnp.sum(folded.T, axis=0, keepdims=True)
+    for step, partner in enumerate(partners):
+        given[step] = jnp.broadcast_to(sums, given.shape[1:])
+        copy = pltpu.make_async_remote_copy(
+            src_ref=given.at[step],
+            dst_ref=got.at[step],
+            send_sem=sends.at[bits + step],
+            recv_sem=lands.at[bits + step],
+            device_id={"psg": partner},
+            device_id_type=pl.DeviceIdType.MESH,
+        )
+        copy.start()
+        copy.wait()
+        sums = sums + got[step][:1]
+    spread = jnp.broadcast_to(sums, (128, sums.shape[1])).T
+    factor = lax.rsqrt(spread / width + epsilon)
+    for c in range(0, projected.shape[1], 128):
+        out_ref[:, c : c + 128] = (
+            projected[:, c : c + 128] * factor * gain_ref[:, c : c + 128]
+        ).astype(jnp.bfloat16)
+
+
+def closing(own_mixed, w_out, norm_gain, shards, width):
+    bits = shards.bit_length() - 1
+    tail_count, columns = own_mixed.shape[0], w_out.shape[1]
+    return pl.pallas_call(
+        functools.partial(closing_kernel, bits, width),
+        out_shape=jax.ShapeDtypeStruct((tail_count, columns), jnp.bfloat16),
+        in_specs=[pl.BlockSpec(memory_space=pltpu.VMEM)] * 3,
+        out_specs=pl.BlockSpec(memory_space=pltpu.VMEM),
+        scratch_shapes=[
+            pltpu.VMEM((shards, *own_mixed.shape), jnp.bfloat16),
+            pltpu.VMEM((tail_count, columns), jnp.float32),
+            pltpu.VMEM((bits, 8, tail_count), jnp.float32),
+            pltpu.VMEM((bits, 8, tail_count), jnp.float32),
+            pltpu.SemaphoreType.DMA((2 * bits,)),
+            pltpu.SemaphoreType.DMA((2 * bits,)),
+        ],
+        compiler_params=pltpu.CompilerParams(
+            collective_id=0, has_side_effects=True, vmem_limit_bytes=32 * 2**20
+        ),
+    )(own_mixed, w_out, norm_gain[None, :])
+
+
+def pair_kernel(slab_ref, key_ref, value_ref, out_ref):
+    both = jnp.concatenate([key_ref[...], value_ref[...]], axis=1)
+    out_ref[0] = jnp.dot(slab_ref[...], both, preferred_element_type=jnp.float32)
+
+
+def pair_products(slab, key_weight, value_weight):
+    count, depth = slab.shape
+    kv_heads = key_weight.shape[1] // HEAD_SIZE
+    column = pl.BlockSpec((depth, HEAD_SIZE), lambda k: (0, k))
+    return pl.pallas_call(
+        pair_kernel,
+        grid=(kv_heads,),
+        out_shape=jax.ShapeDtypeStruct((kv_heads, count, 2 * HEAD_SIZE), jnp.float32),
+        in_specs=[pl.BlockSpec((count, depth), lambda k: (0, 0)), column, column],
+        out_specs=pl.BlockSpec((1, count, 2 * HEAD_SIZE), lambda k: (k, 0, 0)),
+        compiler_params=pltpu.CompilerParams(vmem_limit_bytes=32 * 2**20),
+    )(slab, key_weight, value_weight)
 
 
 def by_heads(
@@ -89,20 +201,16 @@
         w_query.reshape(depth, shards, own_heads * HEAD_SIZE),
         preferred_element_type=jnp.float32,
     )
+    query_part, passage_hidden_states = lax.optimization_barrier(
+        (query_part, passage_hidden_states)
+    )
     query_sum = lax.psum_scatter(query_part, "psg", scatter_dimension=0)
     slab = lax.all_to_all(passage_hidden_states, "psg", 1, 0, tiled=True)
     slab = jnp.concatenate(
         [slab.reshape(share, rows, depth), tail_hidden_states.reshape(share, tail_rows, depth)],
         axis=1,
     )
-    both = jnp.concatenate(
-        [
-            key_weight.reshape(depth, kv_heads, HEAD_SIZE),
-            value_weight.reshape(depth, kv_heads, HEAD_SIZE),
-        ],
-        axis=2,
-    )
-    pair_part = jnp.einsum("rnd,dkc->krnc", slab, both, preferred_element_type=jnp.float32)
+    pair_part = pair_products(slab.reshape(-1, depth), key_weight, value_weight)
     pair_sum = lax.psum_scatter(
         pair_part.reshape(shards, rows + tail_rows, 2 * HEAD_SIZE), "psg", scatter_dimension=0
     )
@@ -151,11 +259,7 @@
     )
     agreed = jnp.sum(numer / denom[..., None], axis=0)
     own_mixed = agreed.reshape(tail_count, own_heads * HEAD_SIZE).astype(jnp.bfloat16)
-    mixed = lax.all_gather(own_mixed, "psg", axis=1, tiled=True)
-    projected = jnp.dot(mixed, w_out, preferred_element_type=jnp.float32)
-    squares = lax.psum(jnp.sum(projected * projected, axis=1), "psg")
-    factor = lax.rsqrt(squares / width + epsilon)[:, None]
-    return (projected * factor * norm_gain[None, :]).astype(jnp.bfloat16)
+    return closing(own_mixed, w_out, norm_gain, shards, width)
 
 
 def by_rows(
@@ -267,6 +371,7 @@
     query_heads = w_query.shape[1] // HEAD_SIZE
     kv_heads = key_weight.shape[1] // HEAD_SIZE
     fits = query_heads % shards == 0 and shards % kv_heads == 0
+    fits = fits and shards & (shards - 1) == 0 and tail_hidden_states.shape[0] % 128 == 0
     if fits and tail_hidden_states.shape[0] % (shards // kv_heads) == 0:
         return by_heads(*arrays)
     return by_rows(*arrays)

time: 307 us -> 273 us (0.89)
  waiting for transfers between devices: 211 us -> 161 us
  Pallas kernels: 0 us -> 32.2 us
  starting transfers between devices: 7.66 us -> 0.08 us
  matrix products: 14.8 us -> 7.87 us
    all_gather x1 -> x0, waiting for transfers between devices: 38.1 us -> none  [by_heads(): mixed = lax.all_gather(own_mixed, 'psg', axis=1, tiled=True)]
    pallas_call x0 -> x2, Pallas kernels: none -> 32.2 us  [the longest x1 30 us: closing(): pl.pallas_call(functools.partial(closing_kernel, bits, width), out_shape=...]
    all_to_all x0 -> x1, blocking collectives: none -> 32.1 us  [by_heads(): slab = lax.all_to_all(passage_hidden_states, 'psg', 1, 0, tiled=True)]
    psum x1 -> x0, blocking collectives: 31.6 us -> none  [by_heads(): squares = lax.psum(jnp.sum(projected * projected, axis=1), 'psg')]
    all_to_all x1 -> x0, waiting for transfers between devices: 21.9 us -> none  [by_heads(): slab = lax.all_to_all(passage_hidden_states, 'psg', 1, 0, tiled=True)]
    reduce_scatter x1, waiting for transfers between devices: 74.7 us -> 83.7 us  [by_heads(): lax.psum_scatter(pair_part.reshape(shards, rows + tail_rows, 2 * HEAD_SIZ...]
    all_to_all x1 -> x0, starting transfers between devices: 7.49 us -> none  [by_heads(): slab = lax.all_to_all(passage_hidden_states, 'psg', 1, 0, tiled=True)]
    dot_general x2 -> x0, matrix products: 6.96 us -> none  [the longest x1 3.62 us: by_heads(): jnp.einsum('rnd,dkc->krnc', slab, both, preferred_element_type=jnp.float32)]
  transfers between devices with their start and end apart: 5 -> 3, of which waited for: 5 -> 3; matrix products, arithmetic and copies ran while one was open for 6% -> 3% of each run, Pallas kernels for 0% -> 0%
where the time goes in v2:
time: 273 us
  waiting for transfers between devices  161 us (59%)
  Pallas kernels  32.2 us (12%)
  blocking collectives  32.1 us (12%)
  local copies, waits for them, and re-layouts  22.6 us (8%)
  between operations  13.4 us (5%)
  matrix products  7.87 us (3%)
  other arithmetic  3.5 us (1%)
    reduce_scatter x1, waiting for transfers between devices, by_heads(): lax.psum_scatter(pair_part.reshape(shards, rows + tail_rows, 2 * HEAD_SIZ...  83.7 us
    reduce_scatter x1, waiting for transfers between devices, by_heads(): query_sum = lax.psum_scatter(query_part, 'psg', scatter_dimension=0)  59.9 us
    all_to_all x1, blocking collectives, by_heads(): slab = lax.all_to_all(passage_hidden_states, 'psg', 1, 0, tiled=True)  32.1 us
    pallas_call x1, Pallas kernels, closing(): pl.pallas_call(functools.partial(closing_kernel, bits, width), out_shape=...  30 us
    all_gather x1, waiting for transfers between devices, by_heads(): every = lax.all_gather(packed, 'psg', axis_index_groups=alike)  16.6 us
    reshape x1, local copies, waits for them, and re-layouts, by_heads(): w_query.reshape(depth, shards, own_heads * HEAD_SIZE)  6.5 us
    reshape x1, local copies, waits for them, and re-layouts, by_heads(): pair_part.reshape(shards, rows + tail_rows, 2 * HEAD_SIZE)  6.22 us
  transfers between devices with their start and end apart: 3, of which 3 were waited for; matrix products, arithmetic and copies ran while one was open for 3% of the time, Pallas kernels for 0%

profile of v2, /device:TPU:0, one launch (start us, length us, event | category | flops | bytes accessed | tf_op | source)
XLA Modules:
  0.0 272.8 jit_solution(4475867896741915667)
XLA Ops:
  6.5 0.0 copy-start.6
  6.5 0.0 reduce-scatter.3.cloned.1.call-start
  6.5 6.5 %copy.96 = bf16[512,4096]{0,1:T(8,128)(2,1)} copy(bf16[512,4096]{1,0:T(8,128)(2,1)} %param.15) | data formatting | bytes 8388608 | tf_op jit(solution)/shard_map/reshape | solution.py:201
  13.0 0.0 copy-done.6
  13.0 0.0 copy-start.5
  13.0 4.9 %convolution_bitcast_fusion = f32[16,128,256]{1,2,0:T(8,128)} fusion(bf16[512,16,256]{0,2,1:T(8,128)(2,1)} %bitcast.74, bf16[128,512]{1,0:T(8,128)(2,1)S(1)} %copy-done.6), kind=kOutput, calls=%fused_computation.5 | convolution fusion | flops 536870912 | bytes 6422528 | tf_op jit(solution)/shard_map/td,dsc->stc/dot_general | solution.py:198
  17.9 0.0 copy-done.5
  17.9 0.1 copy.107
  18.0 0.0 copy-start.2
  18.1 0.0 copy-start.3
  18.1 32.1 %all_to_all.16 = bf16[64,16,512]{2,0,1:T(8,128)(2,1)S(1)} all-to-all(bf16[64,16,512]{2,0,1:T(8,128)(2,1)S(1)} %bitcast.76), channel_id=1, replica_groups=mesh['groups'=2,'psg'=16] {'psg'}, dimensions={1} | all-to-all | bytes 2097152 | tf_op jit(solution)/shard_map/all_to_all | solution.py:208
  50.2 0.1 pad_maximum_fusion
  50.3 0.0 copy-done.2
  50.3 0.0 copy-done.3
  50.3 2.1 shard_map.100
  52.4 0.0 copy-start
  52.5 2.2 copy-done
  54.7 6.2 %copy.82 = f32[16,288,256]{1,2,0:T(8,128)} copy(f32[16,288,256]{2,1,0:T(8,128)} %bitcast.71) | data formatting | bytes 9437184 | tf_op jit(solution)/shard_map/reshape | solution.py:215
  60.9 0.0 reduce-scatter.3.cloned.1.call-update
  60.9 0.0 reduce-scatter.5.cloned.1.call-start
  61.0 0.7 reduce-scatter.5.cloned.1.call-update
  61.7 0.0 all-gather.3.cloned.1.call-start
  61.7 0.0 copy-done.8
  61.7 0.0 copy-done.9
  61.8 0.2 select_reduce_fusion.4
  61.9 0.1 select_reduce_fusion.3
  62.1 0.0 copy-done.7
  62.1 0.1 select_reduce_fusion.2
  62.2 0.1 multiply_reduce_fusion.2
  62.3 0.1 copy.83
  62.4 0.1 fusion.24
  62.5 0.1 select_reduce_fusion
  62.6 0.1 fusion.26
  62.6 0.1 multiply_reduce_fusion.1
  62.7 0.1 multiply_reduce_fusion
  62.9 83.7 %reduce-scatter.3.cloned.1.call-done = f32[1,288,256]{1,2,0:T(8,128)} async-done(((f32[16,288,256]{1,2,0:T(8,128)}), f32[1,288,256]{1,2,0:T(8,128)}) %reduce-scatter.3.cloned.1.call-update) | async-done | bytes 294928 | tf_op jit(solution)/shard_map/reduce_scatter | solution.py:214
  146.6 0.9 slice.67
  147.6 0.9 slice.49
  148.5 0.9 slice.50
  149.5 0.9 fusion.15
  150.4 0.1 pad_maximum_fusion.1
  150.5 0.9 copy.84
  151.4 0.0 all-gather.3.cloned.1.call-update
  151.5 0.3 multiply_cosine_fusion.1
  151.8 59.9 %reduce-scatter.5.cloned.1.call-done = f32[1,128,256]{1,2,0:T(8,128)} async-done(((f32[16,128,256]{1,2,0:T(8,128)}), f32[1,128,256]{1,2,0:T(8,128)}) %reduce-scatter.5.cloned.1.call-update) | async-done | bytes 131088 | tf_op jit(solution)/shard_map/reduce_scatter | solution.py:207
  211.7 0.9 fusion.32
  212.6 0.1 copy.99
  212.7 0.1 copy.98
  212.8 16.6 %all-gather.3.cloned.1.call-done = bf16[4352,128]{1,0:T(8,128)(2,1)} async-done(((bf16[1088,128]{1,0:T(8,128)(2,1)}), bf16[4352,128]{1,0:T(8,128)(2,1)}) %all-gather.3.cloned.1.call-update) | async-done | bytes 1114128 | tf_op jit(solution)/shard_map/all_gather | solution.py:231
  229.4 0.8 fusion.31
  230.2 1.2 slice.54
  231.4 0.3 fusion.33
  231.6 0.1 copy.88
  231.7 0.7 bitcast_reduce_fusion
  232.5 0.7 fusion.1
  233.1 0.0 copy-start.1
  233.1 0.0 copy-start.4
  233.2 1.7 fusion.3
  234.9 0.3 fusion.8
  235.2 0.3 fusion.6
  235.6 0.0 copy-done.1
  235.6 0.0 copy-done.4
  235.6 30.0 %shard_map.101 = bf16[128,512]{1,0:T(8,128)(2,1)S(1)} custom-call(bf16[128,256]{1,0:T(8,128)(2,1)S(1)} %copy_bitcast_fusion.1.own_ref, bf16[4096,512]{1,0:T(8,128)(2,1)S(1)} %copy-done.1, f32[1,512]{1,0:T(1,128)S(1)} %bitcast.73), custom_call_target="tpu_custom_call" | custom-call | tf_op jit(solution)/shard_map/pallas_call | solution.py:135
  265.6 0.7 copy.109
  (23 shorter events, 0.2 us)
Async XLA Ops:
  6.5 6.5 %copy-start.6 = (bf16[128,512]{1,0:T(8,128)(2,1)S(1)}, bf16[128,512]{1,0:T(8,128)(2,1)}, u32[]{:S(2)}) copy-start(bf16[128,512]{1,0:T(8,128)(2,1)} %param.10) | copy-start | bytes 393220
  6.5 140.1 %reduce-scatter.3.cloned.1.call-start = ((), (), s32[]{:S(2)}) async-start(), calls=%async_computation.3 | async-start | bytes 6684672 | tf_op jit(solution)/shard_map/reduce_scatter | solution.py:214
  13.0 4.9 %copy-start.5 = (bf16[64,8192]{1,0:T(8,128)(2,1)S(1)}, bf16[64,8192]{1,0:T(8,128)(2,1)}, u32[]{:S(2)}) copy-start(bf16[64,8192]{1,0:T(8,128)(2,1)} %param.11) | copy-start | bytes 3145732
  18.0 32.2 %copy-start.2 = (bf16[512,512]{1,0:T(8,128)(2,1)S(1)}, bf16[512,512]{1,0:T(8,128)(2,1)}, u32[]{:S(2)}) copy-start(bf16[512,512]{1,0:T(8,128)(2,1)} %key_ref.1) | copy-start | bytes 1572868
  18.1 32.2 %copy-start.3 = (bf16[512,512]{1,0:T(8,128)(2,1)S(1)}, bf16[512,512]{1,0:T(8,128)(2,1)}, u32[]{:S(2)}) copy-start(bf16[512,512]{1,0:T(8,128)(2,1)} %value_ref.1) | copy-start | bytes 1572868
  52.4 2.2 copy-start
  60.9 0.8 copy-start.8
  60.9 0.9 copy-start.9
  60.9 1.2 copy-start.7
  60.9 150.8 %reduce-scatter.5.cloned.1.call-start = ((), (), s32[]{:S(2)}) async-start(), calls=%async_computation.4 | async-start | bytes 2228224 | tf_op jit(solution)/shard_map/reduce_scatter | solution.py:207
  61.7 167.7 %all-gather.3.cloned.1.call-start = ((), (), s32[]{:S(2)}) async-start(), calls=%async_computation.5 | async-start | bytes 1392640 | tf_op jit(solution)/shard_map/all_gather | solution.py:231
  233.1 2.4 copy-start.1
  233.1 2.4 copy-start.4
Sparse Core Ops, SparseCore 0:
  61.0 85.5 reduce-scatter.2
  150.8 60.8 reduce-scatter.4
  213.3 16.0 all-gather.2

commit v3 on v2

--- a/solution.py
+++ b/solution.py
@@ -211,6 +211,7 @@
         axis=1,
     )
     pair_part = pair_products(slab.reshape(-1, depth), key_weight, value_weight)
+    query_sum, pair_part = lax.optimization_barrier((query_sum, pair_part))
     pair_sum = lax.psum_scatter(
         pair_part.reshape(shards, rows + tail_rows, 2 * HEAD_SIZE), "psg", scatter_dimension=0
     )

time: 273 us -> 241 us (0.88)
  waiting for transfers between devices: 161 us -> 126 us
  local copies, waits for them, and re-layouts: 22.6 us -> 25.7 us
    reduce_scatter x1, waiting for transfers between devices: 59.9 us -> 27.3 us  [by_heads(): query_sum = lax.psum_scatter(query_part, 'psg', scatter_dimension=0)]
    unnamed x23 -> x25, local copies, waits for them, and re-layouts: 3.1 us -> 7 us
  transfers between devices with their start and end apart: 3 -> 3, of which waited for: 3 -> 3; matrix products, arithmetic and copies ran while one was open for 3% -> 1% of each run, Pallas kernels for 0% -> 1%
where the time goes in v3:
time: 241 us
  waiting for transfers between devices  126 us (52%)
  blocking collectives  32.1 us (13%)
  Pallas kernels  32.1 us (13%)
  local copies, waits for them, and re-layouts  25.7 us (11%)
  between operations  13.4 us (6%)
  matrix products  7.6 us (3%)
  other arithmetic  3.51 us (1%)
    reduce_scatter x1, waiting for transfers between devices, by_heads(): lax.psum_scatter(pair_part.reshape(shards, rows + tail_rows, 2 * HEAD_SIZ...  82.6 us
    all_to_all x1, blocking collectives, by_heads(): slab = lax.all_to_all(passage_hidden_states, 'psg', 1, 0, tiled=True)  32.1 us
    pallas_call x1, Pallas kernels, closing(): pl.pallas_call(functools.partial(closing_kernel, bits, width), out_shape=...  30 us
    reduce_scatter x1, waiting for transfers between devices, by_heads(): query_sum = lax.psum_scatter(query_part, 'psg', scatter_dimension=0)  27.3 us
    all_gather x1, waiting for transfers between devices, by_heads(): every = lax.all_gather(packed, 'psg', axis_index_groups=alike)  16 us
    unnamed x25, local copies, waits for them, and re-layouts  7 us
    reshape x1, local copies, waits for them, and re-layouts, by_heads(): w_query.reshape(depth, shards, own_heads * HEAD_SIZE)  6.5 us
    reshape x1, local copies, waits for them, and re-layouts, by_heads(): pair_part.reshape(shards, rows + tail_rows, 2 * HEAD_SIZE)  6.22 us
  transfers between devices with their start and end apart: 3, of which 3 were waited for; matrix products, arithmetic and copies ran while one was open for 1% of the time, Pallas kernels for 1%

profile of v3, /device:TPU:0, one launch (start us, length us, event | category | flops | bytes accessed | tf_op | source)
XLA Modules:
  0.0 240.5 jit_solution(12164941080460363050)
XLA Ops:
  6.5 0.0 copy-start.6
  6.5 0.0 reduce-scatter.3.cloned.1.call-start
  6.5 6.5 %copy.96 = bf16[512,4096]{0,1:T(8,128)(2,1)} copy(bf16[512,4096]{1,0:T(8,128)(2,1)} %param.15) | data formatting | bytes 8388608 | tf_op jit(solution)/shard_map/reshape | solution.py:201
  13.0 0.0 copy-done.6
  13.0 4.8 %convolution_bitcast_fusion = f32[16,128,256]{1,2,0:T(8,128)} fusion(bf16[512,16,256]{0,2,1:T(8,128)(2,1)} %bitcast.75, bf16[128,512]{1,0:T(8,128)(2,1)S(1)} %copy-done.6), kind=kOutput, calls=%fused_computation.5 | convolution fusion | flops 536870912 | bytes 6422528 | tf_op jit(solution)/shard_map/td,dsc->stc/dot_general | solution.py:198
  17.8 0.0 reduce-scatter.3.cloned.1.call-update
  17.8 0.0 reduce-scatter.5.cloned.1.call-start
  17.9 1.1 copy-done.5
  19.0 0.1 copy.107
  19.1 0.0 copy-start.2
  19.2 0.0 copy-start.3
  19.2 32.1 %all_to_all.16 = bf16[64,16,512]{2,0,1:T(8,128)(2,1)S(1)} all-to-all(bf16[64,16,512]{2,0,1:T(8,128)(2,1)S(1)} %bitcast.77), channel_id=1, replica_groups=mesh['groups'=2,'psg'=16] {'psg'}, dimensions={1} | all-to-all | bytes 2097152 | tf_op jit(solution)/shard_map/all_to_all | solution.py:208
  51.3 0.1 pad_maximum_fusion
  51.4 0.0 copy-done.2
  51.4 0.0 copy-done.3
  51.4 2.1 shard_map.100
  53.6 0.0 copy-start
  53.6 2.2 copy-done
  55.8 27.3 %reduce-scatter.3.cloned.1.call-done = f32[1,128,256]{1,2,0:T(8,128)} async-done(((f32[16,128,256]{1,2,0:T(8,128)}), f32[1,128,256]{1,2,0:T(8,128)}) %reduce-scatter.3.cloned.1.call-update) | async-done | bytes 131088 | tf_op jit(solution)/shard_map/reduce_scatter | solution.py:207
  83.1 6.2 %copy.82 = f32[16,288,256]{1,2,0:T(8,128)} copy(f32[16,288,256]{2,1,0:T(8,128)} %bitcast.72) | data formatting | bytes 9437184 | tf_op jit(solution)/shard_map/reshape | solution.py:216
  89.3 0.0 reduce-scatter.5.cloned.1.call-update
  89.3 0.0 copy-start.7
  89.3 0.0 all-gather.3.cloned.1.call-start
  89.4 0.6 copy-done.8
  90.0 0.0 copy-done.9
  90.0 0.1 select_reduce_fusion.2
  90.1 0.1 multiply_reduce_fusion.2
  90.2 0.1 copy.83
  90.3 0.0 copy-done.10
  90.3 0.2 select_reduce_fusion.4
  90.5 0.1 select_reduce_fusion.3
  90.6 0.1 fusion.24
  90.7 0.1 select_reduce_fusion
  90.8 0.1 fusion.26
  90.9 0.1 multiply_reduce_fusion.1
  90.9 0.1 multiply_reduce_fusion
  91.1 82.6 %reduce-scatter.5.cloned.1.call-done = f32[1,288,256]{1,2,0:T(8,128)} async-done(((f32[16,288,256]{1,2,0:T(8,128)}), f32[1,288,256]{1,2,0:T(8,128)}) %reduce-scatter.5.cloned.1.call-update) | async-done | bytes 294928 | tf_op jit(solution)/shard_map/reduce_scatter | solution.py:215
  173.7 0.9 slice.67
  174.7 0.9 slice.50
  175.6 0.9 slice.49
  176.6 0.9 fusion.15
  177.6 0.1 pad_maximum_fusion.1
  177.7 0.9 copy.84
  178.5 0.0 all-gather.3.cloned.1.call-update
  178.6 0.3 multiply_cosine_fusion.1
  178.9 0.0 copy-done.7
  178.9 0.1 copy.99
  179.0 0.1 copy.98
  179.2 16.0 %all-gather.3.cloned.1.call-done = bf16[4352,128]{1,0:T(8,128)(2,1)} async-done(((bf16[1088,128]{1,0:T(8,128)(2,1)}), bf16[4352,128]{1,0:T(8,128)(2,1)}) %all-gather.3.cloned.1.call-update) | async-done | bytes 1114128 | tf_op jit(solution)/shard_map/all_gather | solution.py:232
  195.2 0.8 fusion.31
  196.0 1.2 slice.54
  197.2 0.7 bitcast_reduce_fusion
  197.9 0.3 fusion.33
  198.1 0.7 fusion.1
  198.8 0.0 copy-start.4
  198.8 1.6 fusion.3
  200.4 0.1 copy.88
  200.5 0.3 fusion.8
  200.8 0.3 fusion.6
  201.2 0.0 copy-done.4
  201.2 0.0 copy-start.1
  201.2 2.2 copy-done.1
  203.4 30.0 %shard_map.101 = bf16[128,512]{1,0:T(8,128)(2,1)S(1)} custom-call(bf16[128,256]{1,0:T(8,128)(2,1)S(1)} %copy_bitcast_fusion.1.own_ref, bf16[4096,512]{1,0:T(8,128)(2,1)S(1)} %copy-done.1, f32[1,512]{1,0:T(1,128)S(1)} %bitcast.74), custom_call_target="tpu_custom_call" | custom-call | tf_op jit(solution)/shard_map/pallas_call | solution.py:135
  233.4 0.7 copy.109
  (25 shorter events, 0.2 us)
Async XLA Ops:
  6.5 6.5 %copy-start.6 = (bf16[128,512]{1,0:T(8,128)(2,1)S(1)}, bf16[128,512]{1,0:T(8,128)(2,1)}, u32[]{:S(2)}) copy-start(bf16[128,512]{1,0:T(8,128)(2,1)} %param.10) | copy-start | bytes 393220
  6.5 76.5 %reduce-scatter.3.cloned.1.call-start = ((), (), s32[]{:S(2)}) async-start(), calls=%async_computation.3 | async-start | bytes 2228224 | tf_op jit(solution)/shard_map/reduce_scatter | solution.py:207
  17.8 1.2 copy-start.5
  17.8 155.9 %reduce-scatter.5.cloned.1.call-start = ((), (), s32[]{:S(2)}) async-start(), calls=%async_computation.4 | async-start | bytes 6684672 | tf_op jit(solution)/shard_map/reduce_scatter | solution.py:215
  19.1 32.2 %copy-start.2 = (bf16[512,512]{1,0:T(8,128)(2,1)S(1)}, bf16[512,512]{1,0:T(8,128)(2,1)}, u32[]{:S(2)}) copy-start(bf16[512,512]{1,0:T(8,128)(2,1)} %key_ref.1) | copy-start | bytes 1572868
  19.2 32.2 %copy-start.3 = (bf16[512,512]{1,0:T(8,128)(2,1)S(1)}, bf16[512,512]{1,0:T(8,128)(2,1)}, u32[]{:S(2)}) copy-start(bf16[512,512]{1,0:T(8,128)(2,1)} %value_ref.1) | copy-start | bytes 1572868
  53.6 2.2 copy-start
  89.3 0.7 copy-start.8
  89.3 0.7 copy-start.9
  89.3 1.0 copy-start.10
  89.3 89.6 %copy-start.7 = (f32[1,128,256]{1,2,0:T(8,128)S(1)}, f32[1,128,256]{1,2,0:T(8,128)}, u32[]{:S(2)}) copy-start(f32[1,128,256]{1,2,0:T(8,128)} %reduce-scatter.3.cloned.1.call-done) | copy-start | bytes 393220
  89.3 105.8 %all-gather.3.cloned.1.call-start = ((), (), s32[]{:S(2)}) async-start(), calls=%async_computation.5 | async-start | bytes 1392640 | tf_op jit(solution)/shard_map/all_gather | solution.py:232
  198.8 2.4 copy-start.4
  201.2 2.2 copy-start.1
Sparse Core Ops, SparseCore 0:
  18.0 65.0 reduce-scatter.2
  89.5 84.2 reduce-scatter.4
  178.7 16.4 all-gather.2
